TPU v7x, 32 devices: a whole 2x2x4 slice. The times are simulated.
32 devices in a mesh: axial: 8 (over z, y), azim: 4 (over x, core).
Axes of the slice: x: 2, y: 2, z: 4, core: 2. Of those that a mesh axis runs over, the one named last changes fastest.
Arguments:
- tet_state: bfloat16 [175, 32768], P(None, ('axial', 'azim')), may hold values from -6 to 6
- prism_state: bfloat16 [375, 32768], P(None, ('axial', 'azim')), may hold values from -6 to 6
- tet_volume: bfloat16 [175, 175], replicated, may hold values from -0.4375 to 0.4375
- prism_volume: bfloat16 [375, 375], replicated, may hold values from -0.3125 to 0.3125
- face_extrap: bfloat16 [300, 175], replicated, may hold values from -0.4375 to 0.4375
- face_lift: bfloat16 [175, 300], replicated, may hold values from -0.75 to 0.75
- wall_extrap: bfloat16 [75, 375], replicated, may hold values from -0.3125 to 0.3125
- wall_lift: bfloat16 [375, 75], replicated, may hold values from -0.75 to 0.75
- face_code: int32 [32768], P(('axial', 'azim')), may hold values from 0 to 4095, as said below
- face_count: int32 [32, 2], P(('axial', 'azim')), may hold values from 0 to 512, as said below
- face_area: float32 [32768], P(('axial', 'azim')), may hold values from 0.5 to 2
- burn_prism: int32 [16384], P(('axial', 'azim')), may hold values from 0 to 1023, as said below
- burn_owner: int32 [16384, 1], P(('axial', 'azim')), may hold values from 0 to 3; in each aligned block of 512 rows (0 to 511, 512 to 1023, ...) at most 128 rows name the same one
- burn_law: float32 [8, 4, 6], P('axial'), may hold values from 0.5 to 2
Outputs:
- tet_new: bfloat16 [175, 32768], P(None, ('axial', 'azim'))
- prism_new: bfloat16 [375, 32768], P(None, ('axial', 'azim'))
Inputs may be any that keep to these rules, and one draw needn't show every extreme that they name: `face_code`: within each partition's block of 1024 entries the codes are distinct; the first 512 are faces shared with the lower axial neighbour, the rest with the upper; upper slot s of (a, z) is the same face as lower slot s of (a+1, z). `face_count`: column 0 counts live lower slots, column 1 live upper slots; the upper count of (a, z) equals the lower count of (a+1, z); zero at the two ends of the axial range, 1 or more elsewhere; 512 is reached. `burn_prism`: distinct within each partition's block. `burn_owner`: at most 128 wall faces of one partition name one owner, and that bound is reached.
All inputs are finite; a program needn't handle non-finite values.
Results may differ from a plain program's by a relative error of at most 0.0043.
Values may be sent and summed in bfloat16 or wider, within the bound.
A program may use at most 64 MiB of HBM per device.

v0:
```python
import functools

import jax
import jax.numpy as jnp
from jax import lax
from jax.experimental import pallas as pl
from jax.experimental.pallas import tpu as pltpu
from jax.sharding import PartitionSpec as P

NV = 5
TFP = 15
FACES = 4
FACE_PAD = 80
VAR_PAD = 16
OWNER_ROWS = 8
CHUNK = 256
VMEM_LIMIT = 63 * 1024 * 1024

section_step = 0.25
F32 = jnp.float32
BF16 = jnp.bfloat16


def dot(left, right):
    return jnp.dot(left, right, preferred_element_type=F32)


def dot_t(left, right):
    return lax.dot_general(left, right, (((1,), (1,)), ((), ())), preferred_element_type=F32)


def square_half(values):
    widened = values.astype(F32)
    return (0.5 * widened * widened).astype(BF16)


def spread(groups, width, padded):
    row = lax.broadcasted_iota(jnp.int32, (groups * padded, groups * width), 0)
    column = lax.broadcasted_iota(jnp.int32, (groups * padded, groups * width), 1)
    group = jnp.zeros_like(row)
    for g in range(1, groups):
        group = group + (row >= g * padded).astype(jnp.int32)
    hit = (column == row - group * (padded - width)) & (row - group * padded < width)
    return jnp.where(hit, 1.0, 0.0).astype(BF16)


def one_hot(index, base, rows):
    row = lax.broadcasted_iota(jnp.int32, (rows, index.shape[1]), 0) + base
    return jnp.where(row == index, 1.0, 0.0).astype(BF16)


def load_all(pairs, sem):
    loads = [
        pltpu.make_async_copy(source, target, sem.at[i])
        for i, (source, target) in enumerate(pairs)
    ]
    for load in loads:
        load.start()
    return loads


def exchange(
    n_axial,
    n_azim,
    tet_hbm,
    prism_hbm,
    tet_volume_hbm,
    prism_volume_hbm,
    face_extrap_hbm,
    face_lift_hbm,
    wall_extrap_hbm,
    wall_lift_hbm,
    code_hbm,
    burn_hbm,
    owner_hbm,
    law_hbm,
    left_hbm,
    right_hbm,
    base_hbm,
    lift_hbm,
    prism_new_hbm,
    tet_ref,
    prism_ref,
    tet_volume,
    prism_volume,
    face_extrap,
    face_lift,
    wall_extrap,
    wall_lift,
    code_ref,
    burn_ref,
    owner_ref,
    law_ref,
    send,
    tet_base,
    lift,
    prism_new,
    hot,
    prism_base,
    part,
    parts,
    load_sem,
    store_sem,
    send_sem,
    recv_sem,
    part_send_sem,
    part_recv_sem,
):
    axial = lax.axis_index("axial")
    azim = lax.axis_index("azim")
    has_low = axial > 0
    has_high = axial < n_axial - 1
    low = (jnp.maximum(axial - 1, 0), azim)
    high = (jnp.minimum(axial + 1, n_axial - 1), azim)
    others = [(axial, lax.rem(azim + d, n_azim)) for d in range(1, n_azim)]
    mesh_id = pl.DeviceIdType.MESH

    loads = load_all(
        (
            (face_extrap_hbm, face_extrap),
            (code_hbm, code_ref),
            (tet_hbm, tet_ref),
            (burn_hbm, burn_ref),
            (owner_hbm, owner_ref),
            (wall_extrap_hbm, wall_extrap),
            (prism_hbm, prism_ref),
            (prism_volume_hbm, prism_volume),
            (tet_volume_hbm, tet_volume),
            (face_lift_hbm, face_lift),
            (wall_lift_hbm, wall_lift),
            (law_hbm, law_ref),
        ),
        load_sem,
    )
    barrier = pltpu.get_barrier_semaphore()

    @pl.when(has_low)
    def _():
        pl.semaphore_signal(barrier, inc=1, device_id=low, device_id_type=mesh_id)

    @pl.when(has_high)
    def _():
        pl.semaphore_signal(barrier, inc=1, device_id=high, device_id_type=mesh_id)

    for other in others:
        pl.semaphore_signal(barrier, inc=1, device_id=other, device_id_type=mesh_id)

    prisms = prism_ref.shape[1]
    tets, slots = hot.shape
    half = slots // 2
    faces_spread = spread(FACES, face_extrap.shape[1] // FACES, FACE_PAD)
    wall_spread = spread(NV, TFP, VAR_PAD)

    def face_copy(side, device):
        return pltpu.make_async_remote_copy(
            src_ref=send.at[side],
            dst_ref=right_hbm.at[1 - side],
            send_sem=send_sem.at[side],
            recv_sem=recv_sem.at[1 - side],
            device_id=device,
            device_id_type=mesh_id,
        )

    loads[0].wait()
    extrap = dot_t(faces_spread, face_extrap[...]).astype(BF16)
    loads[1].wait()
    code = code_ref[...]
    tet_index = code // FACES
    face = code - FACES * tet_index
    for side in range(2):
        lanes = slice(side * half, (side + 1) * half)
        for base in range(0, tets, CHUNK):
            hot[base : base + CHUNK, lanes] = one_hot(tet_index[:, lanes], base, CHUNK)
        if side == 0:
            loads[2].wait()
        columns = dot(tet_ref[...], hot[:, lanes]).astype(BF16)
        extended = dot(extrap, columns)
        rows = extended[0:FACE_PAD]
        for f in range(1, FACES):
            rows = jnp.where(
                face[:, lanes] == f, extended[f * FACE_PAD : (f + 1) * FACE_PAD], rows
            )
        send[side] = rows.astype(BF16)
        if side == 0:

            @pl.when(has_low & has_high)
            def _():
                pl.semaphore_wait(barrier, n_azim + 1)

            @pl.when(jnp.logical_not(has_low & has_high))
            def _():
                pl.semaphore_wait(barrier, n_azim)

        @pl.when(has_high if side else has_low)
        def _():
            face_copy(side, high if side else low).start()

    for load in loads[3:7]:
        load.wait()
    wall_out = dot(wall_spread, wall_extrap[...]).astype(BF16)
    wall_rows = dot(wall_out, prism_ref[...]).astype(BF16).astype(F32)
    squares = wall_rows[(NV - 1) * VAR_PAD : NV * VAR_PAD]
    squares = squares * squares
    owner_row = lax.broadcasted_iota(jnp.int32, (OWNER_ROWS, owner_ref.shape[1]), 0)
    owner_hot = jnp.where(owner_row == owner_ref[...], 1.0, 0.0).astype(BF16)
    owned = dot_t(owner_hot, one_hot(burn_ref[...], 0, prisms))
    partial = jnp.sum(owned * jnp.sum(squares, axis=0, keepdims=True), axis=1, keepdims=True)
    part[...] = jnp.broadcast_to(partial, part.shape)

    def part_copy(source, d):
        return pltpu.make_async_remote_copy(
            src_ref=part,
            dst_ref=parts.at[source],
            send_sem=part_send_sem.at[d],
            recv_sem=part_recv_sem.at[source],
            device_id=others[d],
            device_id_type=mesh_id,
        )

    for d in range(n_azim - 1):
        part_copy(azim, d).start()

    for load in loads[7:]:
        load.wait()
    tet_state = tet_ref[...]
    tet_base[...] = tet_state.astype(F32) - section_step * dot(
        tet_volume[...], square_half(tet_state)
    )
    lift[...] = dot_t(face_lift[...], faces_spread).astype(BF16)
    stores = load_all(
        ((send, left_hbm), (tet_base, base_hbm), (lift, lift_hbm)), store_sem
    )
    wall_in = lax.dot_general(
        wall_lift[...], wall_spread, (((0,), (1,)), ((), ())), preferred_element_type=F32
    ).astype(BF16)
    for first in range(0, prisms, half):
        lanes = slice(first, first + half)
        state = prism_ref[:, lanes]
        prism_base[:, lanes] = state.astype(F32) - section_step * dot(
            prism_volume[...], square_half(state)
        )

    sums = part[...]
    for d in range(n_azim - 1):
        part_copy(azim, d).wait_send()
        source = others[d][1]
        part_copy(source, d).wait_recv()
        sums = sums + parts[source]
    faces = owner_ref.shape[1]
    inject = [jnp.zeros((1, prisms), F32) for _ in range(NV)]
    walls = jnp.zeros((1, prisms), F32)
    for o in range(n_azim):
        burn = law_ref[o : o + 1, 0:1]
        damping = 1.0 / (1.0 + burn * sums[o : o + 1, 0:1] / (faces * TFP))
        scale = owned[o : o + 1] * (burn * damping)
        walls = walls + owned[o : o + 1]
        for v in range(NV):
            inject[v] = inject[v] + law_ref[o : o + 1, 1 + v : 2 + v] * scale
    wall_jump = jnp.concatenate(
        [
            jnp.where(
                walls > 0.5,
                inject[v] * squares - wall_rows[v * VAR_PAD : (v + 1) * VAR_PAD],
                0.0,
            ).astype(BF16)
            for v in range(NV)
        ],
        axis=0,
    )
    for first in range(0, prisms, half):
        lanes = slice(first, first + half)
        lifted = dot(wall_in, wall_jump[:, lanes])
        prism_new[:, lanes] = (prism_base[:, lanes] - section_step * lifted).astype(BF16)
    last = pltpu.make_async_copy(prism_new, prism_new_hbm, store_sem.at[len(stores)])
    last.start()

    @pl.when(has_low)
    def _():
        face_copy(0, low).wait_send()
        face_copy(1, low).wait_recv()

    @pl.when(has_high)
    def _():
        face_copy(1, high).wait_send()
        face_copy(0, high).wait_recv()

    for store in stores:
        store.wait()
    last.wait()


def finish(
    code_hbm,
    count_hbm,
    area_hbm,
    left_hbm,
    right_hbm,
    base_hbm,
    lift_hbm,
    prism_new_hbm,
    tet_out,
    prism_out,
    code_ref,
    count_ref,
    area_ref,
    left_ref,
    right_ref,
    tet_base,
    lift,
    prism_new,
    tet_new,
    hot,
    load_sem,
    store_sem,
):
    loads = load_all(
        (
            (code_hbm, code_ref),
            (count_hbm, count_ref),
            (area_hbm, area_ref),
            (left_hbm, left_ref),
            (right_hbm, right_ref),
            (lift_hbm, lift),
            (prism_new_hbm, prism_new),
            (base_hbm, tet_base),
        ),
        load_sem,
    )
    tets, slots = hot.shape
    half = slots // 2
    loads[0].wait()
    code = code_ref[...]
    tet_index = code // FACES
    face = code - FACES * tet_index
    for base in range(0, tets, CHUNK):
        hot[base : base + CHUNK, :] = one_hot(tet_index, base, CHUNK)
    for load in loads[1:7]:
        load.wait()
    out_copy = pltpu.make_async_copy(prism_new, prism_out, store_sem.at[0])
    out_copy.start()

    slot = lax.broadcasted_iota(jnp.int32, (1, half), 1)
    jumps = []
    for side in range(2):
        lanes = slice(side * half, (side + 1) * half)
        left = left_ref[side].astype(F32)
        right = right_ref[side].astype(F32)
        speed = jnp.maximum(jnp.abs(left), jnp.abs(right))
        step = right - left
        normal = 0.25 if side else -0.25
        flux_jump = normal * (right * right - left * left) - 0.5 * speed * step
        live = slot < count_ref[0:1, side : side + 1]
        jumps.append(jnp.where(live, area_ref[:, lanes] * flux_jump, 0.0).astype(BF16))
    jump = jnp.concatenate(jumps, axis=1)
    zero = jnp.zeros_like(jump)
    placed = jnp.concatenate([jnp.where(face == f, jump, zero) for f in range(FACES)], axis=0)
    on_tets = dot_t(placed, hot[...]).astype(BF16)
    lifted = dot(lift[...], on_tets)
    loads[7].wait()
    tet_new[...] = (tet_base[...] - section_step * lifted).astype(BF16)
    last = pltpu.make_async_copy(tet_new, tet_out, store_sem.at[1])
    last.start()
    out_copy.wait()
    last.wait()


def on_device(
    n_axial,
    n_azim,
    tet_state,
    prism_state,
    tet_volume,
    prism_volume,
    face_extrap,
    face_lift,
    wall_extrap,
    wall_lift,
    face_code,
    face_count,
    face_area,
    burn_prism,
    burn_owner,
    burn_law,
):
    slots = face_code.shape[0]
    faces = burn_prism.shape[0]
    tets = tet_state.shape[1]
    hbm = pl.BlockSpec(memory_space=pltpu.HBM)
    dma = pltpu.SemaphoreType.DMA

    def vmem(arrays):
        return [pltpu.VMEM(x.shape, x.dtype) for x in arrays]

    code = face_code.reshape(1, slots)
    operands = (
        tet_state,
        prism_state,
        tet_volume,
        prism_volume,
        face_extrap.T,
        face_lift,
        wall_extrap,
        wall_lift.T,
        code,
        burn_prism.reshape(1, faces),
        burn_owner.reshape(1, faces),
        burn_law[0],
    )
    rows = jax.ShapeDtypeStruct((2, FACE_PAD, slots // 2), BF16)
    base = jax.ShapeDtypeStruct(tet_state.shape, F32)
    lift = jax.ShapeDtypeStruct((tet_state.shape[0], FACES * FACE_PAD), BF16)
    prism_new = jax.ShapeDtypeStruct(prism_state.shape, BF16)
    tet_new = jax.ShapeDtypeStruct(tet_state.shape, BF16)
    between = pl.pallas_call(
        functools.partial(exchange, n_axial, n_azim),
        out_shape=(rows, rows, base, lift, prism_new),
        in_specs=[hbm] * len(operands),
        out_specs=[hbm] * 5,
        scratch_shapes=vmem(operands)
        + vmem((rows, base, lift, prism_new))
        + [
            pltpu.VMEM((tets, slots), BF16),
            pltpu.VMEM(prism_state.shape, F32),
            pltpu.VMEM((OWNER_ROWS, 128), F32),
            pltpu.VMEM((n_azim, OWNER_ROWS, 128), F32),
            dma((len(operands),)),
            dma((4,)),
            dma((2,)),
            dma((2,)),
            dma((n_azim - 1,)),
            dma((n_azim,)),
        ],
        compiler_params=pltpu.CompilerParams(
            collective_id=0, has_side_effects=True, vmem_limit_bytes=VMEM_LIMIT
        ),
        name="exchange",
    )(*operands)
    inputs = (code, face_count, face_area.reshape(1, slots)) + tuple(between)
    return pl.pallas_call(
        finish,
        out_shape=(tet_new, prism_new),
        in_specs=[hbm] * len(inputs),
        out_specs=[hbm] * 2,
        scratch_shapes=vmem(inputs[:4])
        + vmem((rows, base, lift, prism_new, tet_new))
        + [pltpu.VMEM((tets, slots), BF16), dma((len(inputs),)), dma((2,))],
        compiler_params=pltpu.CompilerParams(vmem_limit_bytes=VMEM_LIMIT),
        name="finish",
    )(*inputs)


def solution(mesh):
    placed = (
        P(None, ("axial", "azim")),
        P(None, ("axial", "azim")),
        P(),
        P(),
        P(),
        P(),
        P(),
        P(),
        P(("axial", "azim")),
        P(("axial", "azim"), None),
        P(("axial", "azim")),
        P(("axial", "azim")),
        P(("axial", "azim"), None),
        P("axial", None, None),
    )
    return jax.shard_map(
        functools.partial(on_device, mesh.shape["axial"], mesh.shape["azim"]),
        mesh=mesh,
        in_specs=placed,
        out_specs=(P(None, ("axial", "azim")), P(None, ("axial", "azim"))),
        check_vma=False,
    )
```

profile of v0, /device:TPU:0, one launch (start us, length us, event | category | flops | bytes accessed | tf_op | source)
XLA Modules:
  0.0 13.6 jit_solution(1779861636030995039)
XLA Ops:
  0.6 9.5 %exchange.1 = (bf16[2,80,512]{2,1,0:T(8,128)(2,1)}, bf16[2,80,512]{2,1,0:T(8,128)(2,1)}, f32[175,1024]{1,0:T(8,128)}, bf16[175,320]{1,0:T(8,128)(2,1)}, bf16[375,1024]{1,0:T(8,128)(2,1)}) custom-call(bf16[175,1024]{1,0:T(8,128)(2,1)} %tet_hbm.1, bf16[375,1024]{1,0:T(8,128)(2,1)} %prism_hbm.1, bf16[175,175]{1,0:T(8,128)(2,1)} %tet_volume_hbm.1, ...), custom_call_target="tpu_custom_call" | custom-call | tf_op jit(solution)/shard_map/exchange/pallas_call | solution.py:414
  10.2 3.4 %finish.1 = (bf16[175,1024]{1,0:T(8,128)(2,1)}, bf16[375,1024]{1,0:T(8,128)(2,1)}) custom-call(s32[1,1024]{1,0:T(1,128)} %bitcast.10, s32[1,2]{1,0:T(1,128)} %count_hbm.1, f32[1,1024]{1,0:T(1,128)} %bitcast.11, bf16[2,80,512]{2,1,0:T(8,128)(2,1)} %get-tuple-element.7.left_hbm, bf16[2,80,512]{2,1,0:T(8,128)(2,1)} %get-tuple-element.8.right_hbm, ...), custom_call_target="tpu_custom_call" | custom-call | tf_op jit(solution)/shard_map/finish/pallas_call | solution.py:439
where the time goes:
time: 13.8 us; the launch traced here: 13.6 us
  Pallas kernels  13 us (94%)
  between operations  0.64 us (5%)
    pallas_call x1, Pallas kernels, on_device(): pl.pallas_call(functools.partial(exchange, n_axial, n_azim), out_shape=(r...  9.54 us
    pallas_call x1, Pallas kernels, on_device(): pl.pallas_call(finish, out_shape=(tet_new, prism_new), in_specs=[hbm] * l...  3.42 us

commit v1 on v0

--- a/solution.py
+++ b/solution.py
@@ -73,12 +73,15 @@
     code_hbm,
     burn_hbm,
     owner_hbm,
-    law_hbm,
     left_hbm,
     right_hbm,
-    base_hbm,
+    tet_base_hbm,
     lift_hbm,
-    prism_new_hbm,
+    parts_hbm,
+    owned_hbm,
+    wall_rows_hbm,
+    wall_in_hbm,
+    prism_base_hbm,
     tet_ref,
     prism_ref,
     tet_volume,
@@ -90,15 +93,15 @@
     code_ref,
     burn_ref,
     owner_ref,
-    law_ref,
     send,
     tet_base,
     lift,
-    prism_new,
+    owned,
+    wall_rows,
+    wall_in,
+    prism_base,
     hot,
-    prism_base,
     part,
-    parts,
     load_sem,
     store_sem,
     send_sem,
@@ -128,7 +131,6 @@
             (tet_volume_hbm, tet_volume),
             (face_lift_hbm, face_lift),
             (wall_lift_hbm, wall_lift),
-            (law_hbm, law_ref),
         ),
         load_sem,
     )
@@ -198,19 +200,19 @@
     for load in loads[3:7]:
         load.wait()
     wall_out = dot(wall_spread, wall_extrap[...]).astype(BF16)
-    wall_rows = dot(wall_out, prism_ref[...]).astype(BF16).astype(F32)
-    squares = wall_rows[(NV - 1) * VAR_PAD : NV * VAR_PAD]
+    wall_rows[...] = dot(wall_out, prism_ref[...]).astype(BF16)
+    squares = wall_rows[(NV - 1) * VAR_PAD : NV * VAR_PAD, :].astype(F32)
     squares = squares * squares
     owner_row = lax.broadcasted_iota(jnp.int32, (OWNER_ROWS, owner_ref.shape[1]), 0)
     owner_hot = jnp.where(owner_row == owner_ref[...], 1.0, 0.0).astype(BF16)
-    owned = dot_t(owner_hot, one_hot(burn_ref[...], 0, prisms))
-    partial = jnp.sum(owned * jnp.sum(squares, axis=0, keepdims=True), axis=1, keepdims=True)
+    owned[...] = dot_t(owner_hot, one_hot(burn_ref[...], 0, prisms))
+    partial = jnp.sum(owned[...] * jnp.sum(squares, axis=0, keepdims=True), axis=1, keepdims=True)
     part[...] = jnp.broadcast_to(partial, part.shape)
 
     def part_copy(source, d):
         return pltpu.make_async_remote_copy(
             src_ref=part,
-            dst_ref=parts.at[source],
+            dst_ref=parts_hbm.at[source],
             send_sem=part_send_sem.at[d],
             recv_sem=part_recv_sem.at[source],
             device_id=others[d],
@@ -227,52 +229,32 @@
         tet_volume[...], square_half(tet_state)
     )
     lift[...] = dot_t(face_lift[...], faces_spread).astype(BF16)
-    stores = load_all(
-        ((send, left_hbm), (tet_base, base_hbm), (lift, lift_hbm)), store_sem
-    )
-    wall_in = lax.dot_general(
+    wall_in[...] = lax.dot_general(
         wall_lift[...], wall_spread, (((0,), (1,)), ((), ())), preferred_element_type=F32
     ).astype(BF16)
+    stores = load_all(
+        (
+            (part, parts_hbm.at[azim]),
+            (send, left_hbm),
+            (tet_base, tet_base_hbm),
+            (lift, lift_hbm),
+            (owned, owned_hbm),
+            (wall_rows, wall_rows_hbm),
+            (wall_in, wall_in_hbm),
+        ),
+        store_sem,
+    )
     for first in range(0, prisms, half):
         lanes = slice(first, first + half)
         state = prism_ref[:, lanes]
         prism_base[:, lanes] = state.astype(F32) - section_step * dot(
             prism_volume[...], square_half(state)
         )
-
-    sums = part[...]
+    last = pltpu.make_async_copy(prism_base, prism_base_hbm, store_sem.at[len(stores)])
+    last.start()
     for d in range(n_azim - 1):
         part_copy(azim, d).wait_send()
-        source = others[d][1]
-        part_copy(source, d).wait_recv()
-        sums = sums + parts[source]
-    faces = owner_ref.shape[1]
-    inject = [jnp.zeros((1, prisms), F32) for _ in range(NV)]
-    walls = jnp.zeros((1, prisms), F32)
-    for o in range(n_azim):
-        burn = law_ref[o : o + 1, 0:1]
-        damping = 1.0 / (1.0 + burn * sums[o : o + 1, 0:1] / (faces * TFP))
-        scale = owned[o : o + 1] * (burn * damping)
-        walls = walls + owned[o : o + 1]
-        for v in range(NV):
-            inject[v] = inject[v] + law_ref[o : o + 1, 1 + v : 2 + v] * scale
-    wall_jump = jnp.concatenate(
-        [
-            jnp.where(
-                walls > 0.5,
-                inject[v] * squares - wall_rows[v * VAR_PAD : (v + 1) * VAR_PAD],
-                0.0,
-            ).astype(BF16)
-            for v in range(NV)
-        ],
-        axis=0,
-    )
-    for first in range(0, prisms, half):
-        lanes = slice(first, first + half)
-        lifted = dot(wall_in, wall_jump[:, lanes])
-        prism_new[:, lanes] = (prism_base[:, lanes] - section_step * lifted).astype(BF16)
-    last = pltpu.make_async_copy(prism_new, prism_new_hbm, store_sem.at[len(stores)])
-    last.start()
+        part_copy(others[d][1], d).wait_recv()
 
     @pl.when(has_low)
     def _():
@@ -290,25 +272,38 @@
 
 
 def finish(
+    n_azim,
+    faces,
     code_hbm,
     count_hbm,
     area_hbm,
+    law_hbm,
     left_hbm,
     right_hbm,
-    base_hbm,
+    tet_base_hbm,
     lift_hbm,
-    prism_new_hbm,
+    parts_hbm,
+    owned_hbm,
+    wall_rows_hbm,
+    wall_in_hbm,
+    prism_base_hbm,
     tet_out,
     prism_out,
     code_ref,
     count_ref,
     area_ref,
+    law_ref,
     left_ref,
     right_ref,
     tet_base,
     lift,
+    parts,
+    owned,
+    wall_rows,
+    wall_in,
+    prism_base,
+    tet_new,
     prism_new,
-    tet_new,
     hot,
     load_sem,
     store_sem,
@@ -316,28 +311,70 @@
     loads = load_all(
         (
             (code_hbm, code_ref),
-            (count_hbm, count_ref),
-            (area_hbm, area_ref),
             (left_hbm, left_ref),
             (right_hbm, right_ref),
+            (area_hbm, area_ref),
+            (count_hbm, count_ref),
             (lift_hbm, lift),
-            (prism_new_hbm, prism_new),
-            (base_hbm, tet_base),
+            (parts_hbm, parts),
+            (owned_hbm, owned),
+            (wall_rows_hbm, wall_rows),
+            (law_hbm, law_ref),
+            (wall_in_hbm, wall_in),
+            (tet_base_hbm, tet_base),
+            (prism_base_hbm, prism_base),
         ),
         load_sem,
     )
     tets, slots = hot.shape
+    prisms = prism_new.shape[1]
     half = slots // 2
+    stores = []
+
+    def store(new, out, first, width):
+        lanes = pl.ds(first, width)
+        copy = pltpu.make_async_copy(
+            new.at[:, lanes], out.at[:, lanes], store_sem.at[len(stores)]
+        )
+        copy.start()
+        stores.append(copy)
+
     loads[0].wait()
     code = code_ref[...]
     tet_index = code // FACES
     face = code - FACES * tet_index
     for base in range(0, tets, CHUNK):
         hot[base : base + CHUNK, :] = one_hot(tet_index, base, CHUNK)
-    for load in loads[1:7]:
+    for load in loads[1:11]:
         load.wait()
-    out_copy = pltpu.make_async_copy(prism_new, prism_out, store_sem.at[0])
-    out_copy.start()
+
+    sums = parts[0]
+    for source in range(1, n_azim):
+        sums = sums + parts[source]
+    squares = wall_rows[(NV - 1) * VAR_PAD : NV * VAR_PAD, :].astype(F32)
+    squares = squares * squares
+    inject = [jnp.zeros((1, prisms), F32) for _ in range(NV)]
+    walls = jnp.zeros((1, prisms), F32)
+    for o in range(n_azim):
+        burn = law_ref[o : o + 1, 0:1]
+        damping = 1.0 / (1.0 + burn * sums[o : o + 1, 0:1] / (faces * TFP))
+        mine = owned[o : o + 1, :]
+        scale = mine * (burn * damping)
+        walls = walls + mine
+        for v in range(NV):
+            inject[v] = inject[v] + law_ref[o : o + 1, 1 + v : 2 + v] * scale
+    wall_jump = jnp.concatenate(
+        [
+            jnp.where(
+                walls > 0.5,
+                inject[v] * squares
+                - wall_rows[v * VAR_PAD : (v + 1) * VAR_PAD, :].astype(F32),
+                0.0,
+            ).astype(BF16)
+            for v in range(NV)
+        ],
+        axis=0,
+    )
 
     slot = lax.broadcasted_iota(jnp.int32, (1, half), 1)
     jumps = []
@@ -354,14 +391,21 @@
     jump = jnp.concatenate(jumps, axis=1)
     zero = jnp.zeros_like(jump)
     placed = jnp.concatenate([jnp.where(face == f, jump, zero) for f in range(FACES)], axis=0)
-    on_tets = dot_t(placed, hot[...]).astype(BF16)
-    lifted = dot(lift[...], on_tets)
-    loads[7].wait()
-    tet_new[...] = (tet_base[...] - section_step * lifted).astype(BF16)
-    last = pltpu.make_async_copy(tet_new, tet_out, store_sem.at[1])
-    last.start()
-    out_copy.wait()
-    last.wait()
+    lifted = dot(lift[...], placed).astype(BF16)
+    loads[11].wait()
+    loads[12].wait()
+    for first in range(0, prisms, half):
+        lanes = slice(first, first + half)
+        total = prism_base[:, lanes] - section_step * dot(wall_in[...], wall_jump[:, lanes])
+        prism_new[:, lanes] = total.astype(BF16)
+        store(prism_new, prism_out, first, half)
+    for first in range(0, tets, half):
+        lanes = slice(first, first + half)
+        total = tet_base[:, lanes] - section_step * dot_t(lifted, hot[lanes, :])
+        tet_new[:, lanes] = total.astype(BF16)
+        store(tet_new, tet_out, first, half)
+    for copy in stores:
+        copy.wait()
 
 
 def on_device(
@@ -404,27 +448,35 @@
         code,
         burn_prism.reshape(1, faces),
         burn_owner.reshape(1, faces),
-        burn_law[0],
     )
     rows = jax.ShapeDtypeStruct((2, FACE_PAD, slots // 2), BF16)
     base = jax.ShapeDtypeStruct(tet_state.shape, F32)
     lift = jax.ShapeDtypeStruct((tet_state.shape[0], FACES * FACE_PAD), BF16)
     prism_new = jax.ShapeDtypeStruct(prism_state.shape, BF16)
     tet_new = jax.ShapeDtypeStruct(tet_state.shape, BF16)
-    between = pl.pallas_call(
+    between = (
+        rows,
+        rows,
+        base,
+        lift,
+        jax.ShapeDtypeStruct((n_azim, OWNER_ROWS, 128), F32),
+        jax.ShapeDtypeStruct((OWNER_ROWS, prism_state.shape[1]), F32),
+        jax.ShapeDtypeStruct((NV * VAR_PAD, prism_state.shape[1]), BF16),
+        jax.ShapeDtypeStruct((prism_state.shape[0], NV * VAR_PAD), BF16),
+        jax.ShapeDtypeStruct(prism_state.shape, F32),
+    )
+    results = pl.pallas_call(
         functools.partial(exchange, n_axial, n_azim),
-        out_shape=(rows, rows, base, lift, prism_new),
+        out_shape=between,
         in_specs=[hbm] * len(operands),
-        out_specs=[hbm] * 5,
+        out_specs=[hbm] * len(between),
         scratch_shapes=vmem(operands)
-        + vmem((rows, base, lift, prism_new))
+        + vmem((rows, base, lift) + between[5:])
         + [
             pltpu.VMEM((tets, slots), BF16),
-            pltpu.VMEM(prism_state.shape, F32),
             pltpu.VMEM((OWNER_ROWS, 128), F32),
-            pltpu.VMEM((n_azim, OWNER_ROWS, 128), F32),
             dma((len(operands),)),
-            dma((4,)),
+            dma((8,)),
             dma((2,)),
             dma((2,)),
             dma((n_azim - 1,)),
@@ -435,15 +487,15 @@
         ),
         name="exchange",
     )(*operands)
-    inputs = (code, face_count, face_area.reshape(1, slots)) + tuple(between)
+    inputs = (code, face_count, face_area.reshape(1, slots), burn_law[0]) + tuple(results)
     return pl.pallas_call(
-        finish,
+        functools.partial(finish, n_azim, faces),
         out_shape=(tet_new, prism_new),
         in_specs=[hbm] * len(inputs),
         out_specs=[hbm] * 2,
-        scratch_shapes=vmem(inputs[:4])
-        + vmem((rows, base, lift, prism_new, tet_new))
-        + [pltpu.VMEM((tets, slots), BF16), dma((len(inputs),)), dma((2,))],
+        scratch_shapes=vmem(inputs)
+        + vmem((tet_new, prism_new))
+        + [pltpu.VMEM((tets, slots), BF16), dma((len(inputs),)), dma((4,))],
         compiler_params=pltpu.CompilerParams(vmem_limit_bytes=VMEM_LIMIT),
         name="finish",
     )(*inputs)

time: 13.8 us -> 13.1 us (0.949)
  Pallas kernels: 13 us -> 12.2 us
    pallas_call x2, Pallas kernels: 13 us -> 12.2 us  [the longest x1 8.35 us: on_device(): pl.pallas_call(functools.partial(exchange, n_axial, n_azim), out_shape=be...]
where the time goes in v1:
time: 13.1 us; the launch traced here: 12.9 us
  Pallas kernels  12.2 us (93%)
  between operations  0.64 us (5%)
    pallas_call x1, Pallas kernels, on_device(): pl.pallas_call(functools.partial(exchange, n_axial, n_azim), out_shape=be...  8.35 us
    pallas_call x1, Pallas kernels, on_device(): pl.pallas_call(functools.partial(finish, n_azim, faces), out_shape=(tet_n...  3.86 us

profile of v1, /device:TPU:0, one launch (start us, length us, event | category | flops | bytes accessed | tf_op | source)
XLA Modules:
  0.0 12.9 jit_solution(7681100792754300413)
XLA Ops:
  0.6 8.4 %exchange.1 = (bf16[2,80,512]{2,1,0:T(8,128)(2,1)}, bf16[2,80,512]{2,1,0:T(8,128)(2,1)}, f32[175,1024]{1,0:T(8,128)}, bf16[175,320]{1,0:T(8,128)(2,1)}, f32[4,8,...) custom-call(bf16[175,1024]{1,0:T(8,128)(2,1)} %tet_hbm.1, ...), custom_call_target="tpu_custom_call" | custom-call | tf_op jit(solution)/shard_map/exchange/pallas_call | solution.py:468
  9.0 3.9 %finish.1 = (bf16[175,1024]{1,0:T(8,128)(2,1)}, bf16[375,1024]{1,0:T(8,128)(2,1)}) custom-call(s32[1,1024]{1,0:T(1,128)} %bitcast.10, s32[1,2]{1,0:T(1,128)} %count_hbm.1, f32[1,1024]{1,0:T(1,128)} %bitcast.11, f32[4,6]{1,0:T(4,128)} %bitcast.14, bf16[2,80,512]{2,1,0:T(8,128)(2,1)} %get-tuple-element.11.left_hbm, ...), custom_call_target="tpu_custom_call" | custom-call | tf_op jit(solution)/shard_map/finish/pallas_call | solution.py:491

commit v2 on v1

--- a/solution.py
+++ b/solution.py
@@ -120,8 +120,8 @@
 
     loads = load_all(
         (
+            (code_hbm, code_ref),
             (face_extrap_hbm, face_extrap),
-            (code_hbm, code_ref),
             (tet_hbm, tet_ref),
             (burn_hbm, burn_ref),
             (owner_hbm, owner_ref),
@@ -153,37 +153,46 @@
     faces_spread = spread(FACES, face_extrap.shape[1] // FACES, FACE_PAD)
     wall_spread = spread(NV, TFP, VAR_PAD)
 
-    def face_copy(side, device):
+    pieces = half // CHUNK
+
+    def face_copy(side, piece, device):
         return pltpu.make_async_remote_copy(
-            src_ref=send.at[side],
-            dst_ref=right_hbm.at[1 - side],
-            send_sem=send_sem.at[side],
-            recv_sem=recv_sem.at[1 - side],
+            src_ref=send.at[side, piece],
+            dst_ref=right_hbm.at[1 - side, piece],
+            send_sem=send_sem.at[side, piece],
+            recv_sem=recv_sem.at[1 - side, piece],
             device_id=device,
             device_id_type=mesh_id,
         )
 
+    loads[1].wait()
+    extrap = dot_t(faces_spread, face_extrap[...]).astype(BF16)
     loads[0].wait()
-    extrap = dot_t(faces_spread, face_extrap[...]).astype(BF16)
-    loads[1].wait()
     code = code_ref[...]
     tet_index = code // FACES
     face = code - FACES * tet_index
-    for side in range(2):
-        lanes = slice(side * half, (side + 1) * half)
+
+    def of_piece(values, piece):
+        starts = [side * half + piece * CHUNK for side in range(2)]
+        return jnp.concatenate([values[:, start : start + CHUNK] for start in starts], axis=1)
+
+    for piece in range(pieces):
+        lanes = slice(2 * piece * CHUNK, 2 * (piece + 1) * CHUNK)
+        piece_index = of_piece(tet_index, piece)
+        piece_face = of_piece(face, piece)
         for base in range(0, tets, CHUNK):
-            hot[base : base + CHUNK, lanes] = one_hot(tet_index[:, lanes], base, CHUNK)
-        if side == 0:
+            hot[base : base + CHUNK, lanes] = one_hot(piece_index, base, CHUNK)
+        if piece == 0:
             loads[2].wait()
         columns = dot(tet_ref[...], hot[:, lanes]).astype(BF16)
         extended = dot(extrap, columns)
         rows = extended[0:FACE_PAD]
         for f in range(1, FACES):
-            rows = jnp.where(
-                face[:, lanes] == f, extended[f * FACE_PAD : (f + 1) * FACE_PAD], rows
-            )
-        send[side] = rows.astype(BF16)
-        if side == 0:
+            rows = jnp.where(piece_face == f, extended[f * FACE_PAD : (f + 1) * FACE_PAD], rows)
+        rows = rows.astype(BF16)
+        for side in range(2):
+            send[side, piece] = rows[:, side * CHUNK : (side + 1) * CHUNK]
+        if piece == 0:
 
             @pl.when(has_low & has_high)
             def _():
@@ -193,9 +202,13 @@
             def _():
                 pl.semaphore_wait(barrier, n_azim)
 
-        @pl.when(has_high if side else has_low)
+        @pl.when(has_low)
         def _():
-            face_copy(side, high if side else low).start()
+            face_copy(0, piece, low).start()
+
+        @pl.when(has_high)
+        def _():
+            face_copy(1, piece, high).start()
 
     for load in loads[3:7]:
         load.wait()
@@ -258,13 +271,15 @@
 
     @pl.when(has_low)
     def _():
-        face_copy(0, low).wait_send()
-        face_copy(1, low).wait_recv()
+        for piece in range(pieces):
+            face_copy(0, piece, low).wait_send()
+            face_copy(1, piece, low).wait_recv()
 
     @pl.when(has_high)
     def _():
-        face_copy(1, high).wait_send()
-        face_copy(0, high).wait_recv()
+        for piece in range(pieces):
+            face_copy(1, piece, high).wait_send()
+            face_copy(0, piece, high).wait_recv()
 
     for store in stores:
         store.wait()
@@ -345,8 +360,34 @@
     face = code - FACES * tet_index
     for base in range(0, tets, CHUNK):
         hot[base : base + CHUNK, :] = one_hot(tet_index, base, CHUNK)
-    for load in loads[1:11]:
+    for load in loads[1:6]:
         load.wait()
+
+    slot = lax.broadcasted_iota(jnp.int32, (1, CHUNK), 1)
+    jumps = []
+    for side in range(2):
+        for piece in range(half // CHUNK):
+            first = side * half + piece * CHUNK
+            left = left_ref[side, piece].astype(F32)
+            right = right_ref[side, piece].astype(F32)
+            speed = jnp.maximum(jnp.abs(left), jnp.abs(right))
+            step = right - left
+            normal = 0.25 if side else -0.25
+            flux_jump = normal * (right * right - left * left) - 0.5 * speed * step
+            live = slot + piece * CHUNK < count_ref[0:1, side : side + 1]
+            area = area_ref[:, first : first + CHUNK]
+            jumps.append(jnp.where(live, area * flux_jump, 0.0).astype(BF16))
+    jump = jnp.concatenate(jumps, axis=1)
+    zero = jnp.zeros_like(jump)
+    placed = jnp.concatenate([jnp.where(face == f, jump, zero) for f in range(FACES)], axis=0)
+    lifted = dot(lift[...], placed).astype(BF16)
+    for load in loads[6:12]:
+        load.wait()
+    for first in range(0, tets, half):
+        lanes = slice(first, first + half)
+        total = tet_base[:, lanes] - section_step * dot_t(lifted, hot[lanes, :])
+        tet_new[:, lanes] = total.astype(BF16)
+        store(tet_new, tet_out, first, half)
 
     sums = parts[0]
     for source in range(1, n_azim):
@@ -376,34 +417,12 @@
         axis=0,
     )
 
-    slot = lax.broadcasted_iota(jnp.int32, (1, half), 1)
-    jumps = []
-    for side in range(2):
-        lanes = slice(side * half, (side + 1) * half)
-        left = left_ref[side].astype(F32)
-        right = right_ref[side].astype(F32)
-        speed = jnp.maximum(jnp.abs(left), jnp.abs(right))
-        step = right - left
-        normal = 0.25 if side else -0.25
-        flux_jump = normal * (right * right - left * left) - 0.5 * speed * step
-        live = slot < count_ref[0:1, side : side + 1]
-        jumps.append(jnp.where(live, area_ref[:, lanes] * flux_jump, 0.0).astype(BF16))
-    jump = jnp.concatenate(jumps, axis=1)
-    zero = jnp.zeros_like(jump)
-    placed = jnp.concatenate([jnp.where(face == f, jump, zero) for f in range(FACES)], axis=0)
-    lifted = dot(lift[...], placed).astype(BF16)
-    loads[11].wait()
     loads[12].wait()
     for first in range(0, prisms, half):
         lanes = slice(first, first + half)
         total = prism_base[:, lanes] - section_step * dot(wall_in[...], wall_jump[:, lanes])
         prism_new[:, lanes] = total.astype(BF16)
         store(prism_new, prism_out, first, half)
-    for first in range(0, tets, half):
-        lanes = slice(first, first + half)
-        total = tet_base[:, lanes] - section_step * dot_t(lifted, hot[lanes, :])
-        tet_new[:, lanes] = total.astype(BF16)
-        store(tet_new, tet_out, first, half)
     for copy in stores:
         copy.wait()
 
@@ -449,7 +468,7 @@
         burn_prism.reshape(1, faces),
         burn_owner.reshape(1, faces),
     )
-    rows = jax.ShapeDtypeStruct((2, FACE_PAD, slots // 2), BF16)
+    rows = jax.ShapeDtypeStruct((2, slots // 2 // CHUNK, FACE_PAD, CHUNK), BF16)
     base = jax.ShapeDtypeStruct(tet_state.shape, F32)
     lift = jax.ShapeDtypeStruct((tet_state.shape[0], FACES * FACE_PAD), BF16)
     prism_new = jax.ShapeDtypeStruct(prism_state.shape, BF16)
@@ -477,8 +496,8 @@
             pltpu.VMEM((OWNER_ROWS, 128), F32),
             dma((len(operands),)),
             dma((8,)),
-            dma((2,)),
-            dma((2,)),
+            dma(rows.shape[:2]),
+            dma(rows.shape[:2]),
             dma((n_azim - 1,)),
             dma((n_azim,)),
         ],

time: 13.1 us -> 12.9 us (0.985)
    pallas_call x1, Pallas kernels: 3.86 us -> 3.69 us  [on_device(): pl.pallas_call(functools.partial(finish, n_azim, faces), out_shape=(tet_n...]
where the time goes in v2:
time: 12.9 us; the launch traced here: 12.7 us
  Pallas kernels  12.1 us (94%)
  between operations  0.64 us (5%)
    pallas_call x1, Pallas kernels, on_device(): pl.pallas_call(functools.partial(exchange, n_axial, n_azim), out_shape=be...  8.4 us
    pallas_call x1, Pallas kernels, on_device(): pl.pallas_call(functools.partial(finish, n_azim, faces), out_shape=(tet_n...  3.69 us

profile of v2, /device:TPU:0, one launch (start us, length us, event | category | flops | bytes accessed | tf_op | source)
XLA Modules:
  0.0 12.7 jit_solution(17131092429188663836)
XLA Ops:
  0.6 8.4 %exchange.1 = (bf16[2,2,80,256]{3,2,1,0:T(8,128)(2,1)}, bf16[2,2,80,256]{3,2,1,0:T(8,128)(2,1)}, f32[175,1024]{1,0:T(8,128)}, bf16[175,320]{1,0:T(8,128)(2,1)}, ...) custom-call(bf16[175,1024]{1,0:T(8,128)(2,1)} %tet_hbm.1, ...), custom_call_target="tpu_custom_call" | custom-call | tf_op jit(solution)/shard_map/exchange/pallas_call | solution.py:487
  9.0 3.7 %finish.1 = (bf16[175,1024]{1,0:T(8,128)(2,1)}, bf16[375,1024]{1,0:T(8,128)(2,1)}) custom-call(s32[1,1024]{1,0:T(1,128)} %bitcast.10, s32[1,2]{1,0:T(1,128)} %count_hbm.1, f32[1,1024]{1,0:T(1,128)} %bitcast.11, f32[4,6]{1,0:T(4,128)} %bitcast.14, bf16[2,2,80,256]{3,2,1,0:T(8,128)(2,1)} %get-tuple-element.11.left_hbm, ...), custom_call_target="tpu_custom_call" | custom-call | tf_op jit(solution)/shard_map/finish/pallas_call | solution.py:510

commit v3 on v2

--- a/solution.py
+++ b/solution.py
@@ -14,6 +14,7 @@
 VAR_PAD = 16
 OWNER_ROWS = 8
 CHUNK = 256
+PIECE = 128
 VMEM_LIMIT = 63 * 1024 * 1024
 
 section_step = 0.25
@@ -153,7 +154,7 @@
     faces_spread = spread(FACES, face_extrap.shape[1] // FACES, FACE_PAD)
     wall_spread = spread(NV, TFP, VAR_PAD)
 
-    pieces = half // CHUNK
+    pieces = half // PIECE
 
     def face_copy(side, piece, device):
         return pltpu.make_async_remote_copy(
@@ -173,11 +174,11 @@
     face = code - FACES * tet_index
 
     def of_piece(values, piece):
-        starts = [side * half + piece * CHUNK for side in range(2)]
-        return jnp.concatenate([values[:, start : start + CHUNK] for start in starts], axis=1)
+        starts = [side * half + piece * PIECE for side in range(2)]
+        return jnp.concatenate([values[:, start : start + PIECE] for start in starts], axis=1)
 
     for piece in range(pieces):
-        lanes = slice(2 * piece * CHUNK, 2 * (piece + 1) * CHUNK)
+        lanes = slice(2 * piece * PIECE, 2 * (piece + 1) * PIECE)
         piece_index = of_piece(tet_index, piece)
         piece_face = of_piece(face, piece)
         for base in range(0, tets, CHUNK):
@@ -191,7 +192,7 @@
             rows = jnp.where(piece_face == f, extended[f * FACE_PAD : (f + 1) * FACE_PAD], rows)
         rows = rows.astype(BF16)
         for side in range(2):
-            send[side, piece] = rows[:, side * CHUNK : (side + 1) * CHUNK]
+            send[side, piece] = rows[:, side * PIECE : (side + 1) * PIECE]
         if piece == 0:
 
             @pl.when(has_low & has_high)
@@ -263,8 +264,12 @@
         prism_base[:, lanes] = state.astype(F32) - section_step * dot(
             prism_volume[...], square_half(state)
         )
-    last = pltpu.make_async_copy(prism_base, prism_base_hbm, store_sem.at[len(stores)])
-    last.start()
+        there = pl.ds(first, half)
+        copy = pltpu.make_async_copy(
+            prism_base.at[:, there], prism_base_hbm.at[:, there], store_sem.at[len(stores)]
+        )
+        copy.start()
+        stores.append(copy)
     for d in range(n_azim - 1):
         part_copy(azim, d).wait_send()
         part_copy(others[d][1], d).wait_recv()
@@ -283,7 +288,6 @@
 
     for store in stores:
         store.wait()
-    last.wait()
 
 
 def finish(
@@ -363,19 +367,19 @@
     for load in loads[1:6]:
         load.wait()
 
-    slot = lax.broadcasted_iota(jnp.int32, (1, CHUNK), 1)
+    slot = lax.broadcasted_iota(jnp.int32, (1, PIECE), 1)
     jumps = []
     for side in range(2):
-        for piece in range(half // CHUNK):
-            first = side * half + piece * CHUNK
+        for piece in range(half // PIECE):
+            first = side * half + piece * PIECE
             left = left_ref[side, piece].astype(F32)
             right = right_ref[side, piece].astype(F32)
             speed = jnp.maximum(jnp.abs(left), jnp.abs(right))
             step = right - left
             normal = 0.25 if side else -0.25
             flux_jump = normal * (right * right - left * left) - 0.5 * speed * step
-            live = slot + piece * CHUNK < count_ref[0:1, side : side + 1]
-            area = area_ref[:, first : first + CHUNK]
+            live = slot + piece * PIECE < count_ref[0:1, side : side + 1]
+            area = area_ref[:, first : first + PIECE]
             jumps.append(jnp.where(live, area * flux_jump, 0.0).astype(BF16))
     jump = jnp.concatenate(jumps, axis=1)
     zero = jnp.zeros_like(jump)
@@ -468,7 +472,7 @@
         burn_prism.reshape(1, faces),
         burn_owner.reshape(1, faces),
     )
-    rows = jax.ShapeDtypeStruct((2, slots // 2 // CHUNK, FACE_PAD, CHUNK), BF16)
+    rows = jax.ShapeDtypeStruct((2, slots // 2 // PIECE, FACE_PAD, PIECE), BF16)
     base = jax.ShapeDtypeStruct(tet_state.shape, F32)
     lift = jax.ShapeDtypeStruct((tet_state.shape[0], FACES * FACE_PAD), BF16)
     prism_new = jax.ShapeDtypeStruct(prism_state.shape, BF16)
@@ -495,7 +499,7 @@
             pltpu.VMEM((tets, slots), BF16),
             pltpu.VMEM((OWNER_ROWS, 128), F32),
             dma((len(operands),)),
-            dma((8,)),
+            dma((9,)),
             dma(rows.shape[:2]),
             dma(rows.shape[:2]),
             dma((n_azim - 1,)),

time: 12.9 us -> 13.8 us (1.070)
  Pallas kernels: 12.1 us -> 12.9 us
    pallas_call x1, Pallas kernels: 8.4 us -> 9.22 us  [on_device(): pl.pallas_call(functools.partial(exchange, n_axial, n_azim), out_shape=be...]
where the time goes in v3:
time: 13.8 us; the launch traced here: 13.6 us
  Pallas kernels  12.9 us (93%)
  between operations  0.64 us (5%)
    pallas_call x1, Pallas kernels, on_device(): pl.pallas_call(functools.partial(exchange, n_axial, n_azim), out_shape=be...  9.22 us
    pallas_call x1, Pallas kernels, on_device(): pl.pallas_call(functools.partial(finish, n_azim, faces), out_shape=(tet_n...  3.7 us

profile of v3, /device:TPU:0, one launch (start us, length us, event | category | flops | bytes accessed | tf_op | source)
XLA Modules:
  0.0 13.6 jit_solution(10151859759902981816)
XLA Ops:
  0.6 9.2 %exchange.1 = (bf16[2,4,80,128]{3,2,1,0:T(8,128)(2,1)}, bf16[2,4,80,128]{3,2,1,0:T(8,128)(2,1)}, f32[175,1024]{1,0:T(8,128)}, bf16[175,320]{1,0:T(8,128)(2,1)}, ...) custom-call(bf16[175,1024]{1,0:T(8,128)(2,1)} %tet_hbm.1, ...), custom_call_target="tpu_custom_call" | custom-call | tf_op jit(solution)/shard_map/exchange/pallas_call | solution.py:491
  9.9 3.7 %finish.1 = (bf16[175,1024]{1,0:T(8,128)(2,1)}, bf16[375,1024]{1,0:T(8,128)(2,1)}) custom-call(s32[1,1024]{1,0:T(1,128)} %bitcast.10, s32[1,2]{1,0:T(1,128)} %count_hbm.1, f32[1,1024]{1,0:T(1,128)} %bitcast.11, f32[4,6]{1,0:T(4,128)} %bitcast.14, bf16[2,4,80,128]{3,2,1,0:T(8,128)(2,1)} %get-tuple-element.11.left_hbm, ...), custom_call_target="tpu_custom_call" | custom-call | tf_op jit(solution)/shard_map/finish/pallas_call | solution.py:514
